TPU v7x, 32 devices: a whole 2x2x4 slice. The times are simulated.
32 devices in a mesh: groups: 2 (over y), tx: 4 (over z), ty: 2 (over x), sl: 2 (over core).
Axes of the slice: x: 2, y: 2, z: 4, core: 2. Of those that a mesh axis runs over, the one named last changes fastest.
Arguments:
- object_field: float32 [8, 2, 1024, 1024], P(('groups', 'sl'), None, 'tx', 'ty'), parts along dimension 0, may hold values from -1 to 2
- probe_wave: float32 [4, 128, 128], P('groups'), parts along dimension 0, may hold values from -4.2 to 4.2
- measured: float32 [96, 128, 128], P(('groups', 'tx', 'ty')), parts along dimension 0, may hold values from 0.1 to 4
- owner_row: int32 [96, 1], P(('groups', 'tx', 'ty')), parts along dimension 0, may hold values from 0 to 3; in each aligned block of 6 rows (0 to 5, 6 to 11, ...) at most 3 rows name the same one
- list_rows: int32 [8, 2, 4, 3], P(('groups', 'tx'), 'ty'), parts along dimension 0, may hold values from 0 to 128
- list_cols: int32 [8, 2, 4, 3], P(('groups', 'tx'), 'ty'), parts along dimension 0, may hold values from 0 to 384
Outputs:
- object_out: float32 [8, 2, 1024, 1024], P(('groups', 'sl'), None, 'tx', 'ty'), parts along dimension 0
- probe_out: float32 [4, 128, 128], P('groups'), parts along dimension 0
There are 2 independent parts, one for each index of `groups`. A program takes and returns all parts, laid end to end along the dimension named above; each array names one. Nothing has to cross between parts.
Inputs may be any that keep to these rules, and one draw needn't show every extreme that they name: `owner_row`: at most 3 positions of the rows of one device name the same tile row, and some device reaches 3. `list_rows`: entry [o, j, s, k] belongs to the k-th position (in order) of device (s, j) whose tile row is o; entries with k at or past that device's count for o are not read. Every window lies inside one tile. `list_cols`: same order as list_rows.
All inputs are finite; a program needn't handle non-finite values.
Results may differ from a plain program's by a relative error of at most 0.0098.
Values may be sent and summed in bfloat16 or wider, within the bound.
A program may use at most 192 MiB of HBM per device.

v0:
```python
import functools
import math

import jax
import jax.numpy as jnp
import numpy as np
from jax import lax
from jax.experimental import pallas as pl
from jax.experimental.pallas import tpu as pltpu
from jax.sharding import PartitionSpec as P

ITERS = 2
PHASE = 0.25
STEP_OBJECT = 0.01
STEP_PROBE = 0.6
F32 = jnp.float32
BF16 = jnp.bfloat16
MESH = pl.DeviceIdType.MESH


def real_tables(pixels):
    index = np.arange(pixels)
    four = np.exp(-2j * math.pi * ((index[:, None] * index[None, :]) % pixels) / pixels) / math.sqrt(pixels)
    freq = np.where(index < pixels // 2, index, index - pixels).astype(np.float64)
    kern = (np.conj(four) * np.exp(-1j * PHASE * freq * freq / pixels)[None, :]) @ four
    found = []
    for matrix in (kern, four):
        right = np.block([[matrix.real, matrix.imag], [-matrix.imag, matrix.real]])
        found += [right, right.T]
    whole = np.stack(found).astype(np.float32)
    high = whole.astype(jnp.bfloat16)
    low = (whole - high.astype(np.float32)).astype(jnp.bfloat16)
    return np.stack([high, low], axis=1)


def split(x):
    high = x.astype(BF16)
    return high, (x - high.astype(F32)).astype(BF16)


def dot(a, b):
    return jnp.dot(a, b, preferred_element_type=F32)


def loop(count, step):
    if count <= 8:
        for i in range(count):
            step(i)
    else:
        lax.fori_loop(0, count, lambda i, carry: (step(i), carry)[1], 0)


def lanes(i, width):
    return pl.ds(i * width if isinstance(i, int) else pl.multiple_of(i * width, width), width)


def both_sides(x, tabs, right, left, px, fine=True):
    count = x.shape[1] // px

    def rows(v):
        return jnp.concatenate(
            [
                jnp.concatenate([v[:px, s * px : (s + 1) * px], v[px:, s * px : (s + 1) * px]], axis=1)
                for s in range(count)
            ],
            axis=0,
        )

    def columns(v):
        return jnp.concatenate(
            [
                jnp.concatenate([v[s * px : (s + 1) * px, :px], v[s * px : (s + 1) * px, px:]], axis=0)
                for s in range(count)
            ],
            axis=1,
        )

    m_high, m_low = tabs[right, 0], tabs[right, 1]
    if not fine:
        v = rows(x.astype(BF16))
        y = dot(jnp.concatenate([v, v], axis=1), jnp.concatenate([m_high, m_low], axis=0))
        v = columns(y.astype(BF16))
        m_high, m_low = tabs[left, 0], tabs[left, 1]
        return dot(jnp.concatenate([m_high, m_low], axis=1), jnp.concatenate([v, v], axis=0))
    high, low = split(x)
    high, low = rows(high), rows(low)
    y = dot(
        jnp.concatenate([high, low, high], axis=1), jnp.concatenate([m_high, m_high, m_low], axis=0)
    )
    high, low = split(y)
    high, low = columns(high), columns(low)
    m_high, m_low = tabs[left, 0], tabs[left, 1]
    return dot(
        jnp.concatenate([m_high, m_high, m_low], axis=1), jnp.concatenate([high, low, high], axis=0)
    )


def times(a, b, px):
    ar, ai, br, bi = a[:px], a[px:], b[:px], b[px:]
    return jnp.concatenate([ar * br - ai * bi, ar * bi + ai * br], axis=0)


def conj_times(a, g, px):
    ar, ai, gr, gi = a[:px], a[px:], g[:px], g[px:]
    return jnp.concatenate([ar * gr + ai * gi, ar * gi - ai * gr], axis=0)


def kernel(
    n_tx, n_ty, n_sl, cap, all_positions,
    obj, probe, measured, route, tabs,
    obj_out, probe_out,
    tile, pat, staged, cut_r, cut_c, put_r, put_c, patches, phis, grads, g_recv, placed,
    pieces, pg_mine, delta_mine, deltas, wave, pg_sum,
    tile_send, tile_recv, pat_send, pat_recv, g_send, g_rcv, pc_send, pc_recv, dl_send, dl_recv,
):
    ix, iy, core = lax.axis_index("tx"), lax.axis_index("ty"), lax.axis_index("sl")
    layers, _, rows, cols = obj.shape
    positions, px, _ = measured.shape
    half = n_tx // n_sl
    slots = half * cap
    total = n_sl * layers
    other = 1 - core
    devices = n_tx * n_ty * n_sl
    me = (ix * n_ty + iy) * n_sl + core
    peer = {"sl": other}

    def at(i):
        return {"tx": i // (n_ty * n_sl), "ty": (i // n_sl) % n_ty, "sl": i % n_sl}

    barrier = pltpu.get_barrier_semaphore()

    def greet(i, carry):
        @pl.when(i != me)
        def _():
            pl.semaphore_signal(barrier, inc=1, device_id=at(i), device_id_type=MESH)

        return carry

    lax.fori_loop(0, devices, greet, 0)

    for l in range(layers):
        for part in range(2):
            tile[0, core * layers + l, part] = obj[l, part].astype(BF16)
    wave[...] = jnp.concatenate([probe[0], probe[1]], axis=0)

    def stage(o, carry):
        seen = jnp.int32(0)
        found = [jnp.int32(-1)] * cap
        for p in range(positions):
            here = route[0, 2 * n_tx * cap + p] == o
            for k in range(cap):
                found[k] = jnp.where(here & (seen == k), jnp.int32(p), found[k])
            seen = seen + jnp.where(here, 1, 0)
        for k in range(cap):
            values = jnp.full((px, px), -1.0, F32)
            for p in range(positions):
                values = jnp.where(found[k] == p, measured[p], values)
            staged[o, k] = values.astype(BF16)
        return carry

    lax.fori_loop(0, n_tx, stage, 0)
    pl.semaphore_wait(barrier, devices - 1)

    def send_tile(it, l):
        where = tile.at[it, core * layers + l]
        copy = pltpu.make_async_remote_copy(
            src_ref=where, dst_ref=where, send_sem=tile_send.at[it, l], recv_sem=tile_recv.at[it, l],
            device_id=peer, device_id_type=MESH,
        )
        copy.start()

    def tile_copy(it, l):
        where = tile.at[it, other * layers + l]
        return pltpu.make_async_remote_copy(
            src_ref=where, dst_ref=where, send_sem=tile_send.at[it, l], recv_sem=tile_recv.at[it, l],
            device_id=peer, device_id_type=MESH,
        )

    for l in range(layers):
        send_tile(0, l)

    mine_sends = (ix // half) == core
    local_s = lax.rem(ix, half)

    def pattern_copy(o, s):
        return pltpu.make_async_remote_copy(
            src_ref=staged.at[o], dst_ref=pat.at[s], send_sem=pat_send.at[o], recv_sem=pat_recv.at[s],
            device_id={"tx": o}, device_id_type=MESH,
        )

    @pl.when(mine_sends)
    def _():
        def send(o, carry):
            @pl.when(o != ix)
            def _():
                pattern_copy(o, local_s).start()

            return carry

        lax.fori_loop(0, n_tx, send, 0)
        pat[local_s] = staged[ix]

    def slot_corner(t, c):
        s, k = c * half + t // cap, t % cap
        return route[0, s * cap + k], route[0, (n_tx + s) * cap + k]

    def hot(shape, axis, shift):
        long = lax.broadcasted_iota(jnp.int32, shape, axis)
        short = lax.broadcasted_iota(jnp.int32, shape, 1 - axis)
        return jnp.where(long - short == shift, 1.0, 0.0).astype(BF16)

    def build(t):
        row, col = slot_corner(t, core)
        cut_r[t] = hot((px, rows), 1, row)
        cut_c[:, lanes(t, px)] = hot((cols, px), 0, col)
        put_r[t] = hot((rows, px), 0, row)
        put_c[lanes(t, px), :] = hot((px, cols), 1, col)
        row, col = slot_corner(t, other)
        put_r[slots + t] = hot((rows, px), 0, row)
        put_c[lanes(slots + t, px), :] = hot((px, cols), 1, col)

    loop(slots, build)

    group = 2 if slots % 2 == 0 else 1
    chunk = max(d for d in range(1, 7) if slots % d == 0)
    fine_chunk = 2 if chunk % 2 == 0 else 1
    width = fine_chunk * px

    for it in range(ITERS):
        def cut(pair, start):
            held = tile[it, pl.ds(start, layers)].reshape(layers * 2 * rows, cols)
            narrow = dot(held, cut_c[:, lanes(pair, group * px)]).astype(BF16)
            for i in range(group):
                t = pair * group + i
                wide = jnp.concatenate(
                    [narrow[q * rows : (q + 1) * rows, i * px : (i + 1) * px] for q in range(2 * layers)], axis=1
                )
                done = dot(cut_r[t], wide).astype(BF16)
                for q in range(2 * layers):
                    patches[start + q // 2, q % 2 * px : (q % 2 + 1) * px, lanes(t, px)] = (
                        done[:, q * px : (q + 1) * px]
                    )

        loop(slots // group, lambda pair: cut(pair, core * layers))
        for l in range(layers):
            tile_copy(it, l).wait_recv()
        loop(slots // group, lambda pair: cut(pair, other * layers))

        if it > 0:
            finish_probe(it - 1)

        if it == 0:

            def arrive(i, carry):
                @pl.when(core * half + i != ix)
                def _():
                    pattern_copy(ix, i).wait_recv()

                return carry

            lax.fori_loop(0, half, arrive, 0)

        pg_sum[...] = jnp.zeros_like(pg_sum)

        def run(k):
            first = k * chunk
            spans = [lanes(first // fine_chunk + i, width) for i in range(chunk // fine_chunk)]
            w = jnp.concatenate([wave[...]] * fine_chunk, axis=1)
            psi = [times(w, patches[0, :, span].astype(F32), px) for span in spans]
            for l in range(1, total):
                for i, span in enumerate(spans):
                    phi = both_sides(psi[i], tabs, 0, 1, px)
                    phis[l - 1, :, span] = phi
                    psi[i] = times(phi, patches[l, :, span].astype(F32), px)
            g = []
            for i in range(len(spans)):
                far = both_sides(psi[i], tabs, 2, 3, px)
                target = []
                for s in range(fine_chunk):
                    t = first + i * fine_chunk + s
                    target.append(pat[t // cap, t % cap].astype(F32))
                target = jnp.concatenate(target, axis=1)
                fr, fi = far[:px], far[px:]
                miss = jnp.where(target >= 0.0, 2.0 * (fr * fr + fi * fi - target), 0.0)
                g.append(jnp.concatenate([miss * fr, miss * fi], axis=0))
            g = [both_sides(one, tabs, 3, 2, px, fine=False) for one in g]
            for l in range(total - 1, -1, -1):
                for i, span in enumerate(spans):
                    before = phis[l - 1, :, span] if l else w
                    grads[l, :, span] = conj_times(before, g[i], px).astype(BF16)
                    g[i] = conj_times(patches[l, :, span].astype(F32), g[i], px)
                    if l:
                        g[i] = both_sides(g[i], tabs, 1, 0, px, fine=False)
            for one in g:
                for s in range(fine_chunk):
                    pg_sum[...] += one[:, s * px : (s + 1) * px]

        loop(slots // chunk, run)

        def grad_copy(it):
            return pltpu.make_async_remote_copy(
                src_ref=grads.at[pl.ds(other * layers, layers)], dst_ref=g_recv.at[it],
                send_sem=g_send.at[it], recv_sem=g_rcv.at[it], device_id=peer, device_id_type=MESH,
            )

        grad_copy(it).start()
        pg_mine[it] = pg_sum[...].astype(BF16)
        reducers = delta_count(devices, 2 * px)
        deep = 2 * px // reducers

        def piece_copy(it, i, source):
            return pltpu.make_async_remote_copy(
                src_ref=pg_mine.at[it, pl.ds(pl.multiple_of(i * deep, deep), deep)],
                dst_ref=pieces.at[it, source], send_sem=pc_send.at[it, i], recv_sem=pc_recv.at[it, source],
                device_id=at(i), device_id_type=MESH,
            )

        def send_piece(i, carry):
            @pl.when(i != me)
            def _():
                piece_copy(it, i, me).start()

            return carry

        lax.fori_loop(0, reducers, send_piece, 0)

        def spread(t, values):
            placed_now = dot(put_r[t], values).astype(BF16)
            for q in range(2 * layers):
                placed[q, :, lanes(t, px)] = placed_now[:, q * px : (q + 1) * px]

        def spread_own(t):
            spread(t, jnp.concatenate(
                [grads[core * layers + q // 2, q % 2 * px : (q % 2 + 1) * px, lanes(t, px)]
                 for q in range(2 * layers)], axis=1))

        def spread_got(t):
            spread(slots + t, jnp.concatenate(
                [g_recv[it, q // 2, q % 2 * px : (q % 2 + 1) * px, lanes(t, px)]
                 for q in range(2 * layers)], axis=1))

        loop(slots, spread_own)

        def delta_copy(it, i, source):
            where = pl.ds(pl.multiple_of(source * deep, deep), deep)
            return pltpu.make_async_remote_copy(
                src_ref=delta_mine.at[it], dst_ref=deltas.at[it, where],
                send_sem=dl_send.at[it, i], recv_sem=dl_recv.at[it, source],
                device_id=at(i), device_id_type=MESH,
            )

        @pl.when(me < reducers)
        def _():
            own = pl.ds(pl.multiple_of(me * deep, deep), deep)
            pieces[it, me] = pg_mine[it, own]

            def wait_piece(i, carry):
                @pl.when(i != me)
                def _():
                    piece_copy(it, me, i).wait_recv()

                return carry

            lax.fori_loop(0, devices, wait_piece, 0)
            add = lax.fori_loop(
                0, devices, lambda i, acc: acc + pieces[it, i].astype(F32), jnp.zeros((deep, px), F32)
            )
            delta_mine[it] = add.astype(BF16)
            deltas[it, own] = delta_mine[it]

            def send_delta(i, carry):
                @pl.when(i != me)
                def _():
                    delta_copy(it, i, me).start()

                return carry

            lax.fori_loop(0, devices, send_delta, 0)

        def finish_probe(it):
            def wait_delta(i, carry):
                @pl.when(i != me)
                def _():
                    delta_copy(it, me, i).wait_recv()

                return carry

            lax.fori_loop(0, reducers, wait_delta, 0)
            wave[...] -= (STEP_PROBE / all_positions) * deltas[it].astype(F32)

        grad_copy(it).wait_recv()
        loop(slots, spread_got)
        for q in range(2 * layers):
            l, part = q // 2, q % 2
            before = obj[l, part] if it == 0 else obj_out[l, part]
            now = before - STEP_OBJECT * dot(placed[q], put_c[...])
            obj_out[l, part] = now
            if it < ITERS - 1:
                tile[it + 1, core * layers + l, part] = now.astype(BF16)
                if part == 1:
                    send_tile(it + 1, l)
        grad_copy(it).wait_send()

    finish_probe(ITERS - 1)
    probe_out[0] = wave[:px]
    probe_out[1] = wave[px:]

    @pl.when(mine_sends)
    def _():
        def sent(o, carry):
            @pl.when(o != ix)
            def _():
                pattern_copy(o, local_s).wait_send()

            return carry

        lax.fori_loop(0, n_tx, sent, 0)

    for it in range(ITERS):
        for l in range(layers):
            tile_copy(it, l).wait_send()

        def sent_piece(i, carry):
            @pl.when(i != me)
            def _():
                piece_copy(it, i, me).wait_send()

            return carry

        lax.fori_loop(0, reducers, sent_piece, 0)

        @pl.when(me < reducers)
        def _():
            def sent_delta(i, carry):
                @pl.when(i != me)
                def _():
                    delta_copy(it, i, me).wait_send()

                return carry

            lax.fori_loop(0, devices, sent_delta, 0)


def delta_count(devices, rows):
    return min(devices, rows // 16)


def body(object_field, probe_wave, measured, owner_row, list_rows, list_cols):
    layers, _, rows, cols = object_field.shape
    positions, px, _ = measured.shape
    n_tx, n_ty, n_sl = lax.axis_size("tx"), lax.axis_size("ty"), lax.axis_size("sl")
    cap = list_rows.shape[-1]
    half = n_tx // n_sl
    slots = half * cap
    total = n_sl * layers
    devices = n_tx * n_ty * n_sl
    deep = 2 * px // delta_count(devices, 2 * px)
    tabs = jnp.asarray(real_tables(px))
    route = jnp.concatenate([list_rows.reshape(1, -1), list_cols.reshape(1, -1), owner_row.reshape(1, -1)], axis=1)
    vmem = pl.BlockSpec(memory_space=pltpu.VMEM)
    smem = pl.BlockSpec(memory_space=pltpu.SMEM)
    dma = pltpu.SemaphoreType.DMA
    return pl.pallas_call(
        functools.partial(kernel, n_tx, n_ty, n_sl, cap, positions * n_tx * n_ty),
        out_shape=(
            jax.ShapeDtypeStruct(object_field.shape, F32),
            jax.ShapeDtypeStruct(probe_wave.shape, F32),
        ),
        in_specs=[vmem, vmem, vmem, smem, vmem],
        out_specs=(vmem, vmem),
        scratch_shapes=[
            pltpu.VMEM((ITERS, total, 2, rows, cols), BF16),
            pltpu.VMEM((half, cap, px, px), BF16),
            pltpu.VMEM((n_tx, cap, px, px), BF16),
            pltpu.VMEM((slots, px, rows), BF16),
            pltpu.VMEM((cols, slots * px), BF16),
            pltpu.VMEM((2 * slots, rows, px), BF16),
            pltpu.VMEM((2 * slots * px, cols), BF16),
            pltpu.VMEM((total, 2 * px, slots * px), BF16),
            pltpu.VMEM((total - 1, 2 * px, slots * px), F32),
            pltpu.VMEM((total, 2 * px, slots * px), BF16),
            pltpu.VMEM((ITERS, layers, 2 * px, slots * px), BF16),
            pltpu.VMEM((2 * layers, rows, 2 * slots * px), BF16),
            pltpu.VMEM((ITERS, devices, deep, px), BF16),
            pltpu.VMEM((ITERS, 2 * px, px), BF16),
            pltpu.VMEM((ITERS, deep, px), BF16),
            pltpu.VMEM((ITERS, 2 * px, px), BF16),
            pltpu.VMEM((2 * px, px), F32),
            pltpu.VMEM((2 * px, px), F32),
            dma((ITERS, layers)),
            dma((ITERS, layers)),
            dma((n_tx,)),
            dma((half,)),
            dma((ITERS,)),
            dma((ITERS,)),
            dma((ITERS, devices)),
            dma((ITERS, devices)),
            dma((ITERS, devices)),
            dma((ITERS, devices)),
        ],
        compiler_params=pltpu.CompilerParams(
            collective_id=0, has_side_effects=True, vmem_limit_bytes=58 * 2**20
        ),
    )(object_field, probe_wave, measured, route, tabs)


def solution(mesh):
    in_specs = (
        P(("groups", "sl"), None, "tx", "ty"),
        P("groups", None, None),
        P(("groups", "tx", "ty"), None, None),
        P(("groups", "tx", "ty"), None),
        P(("groups", "tx"), "ty", None, None),
        P(("groups", "tx"), "ty", None, None),
    )
    out_specs = (P(("groups", "sl"), None, "tx", "ty"), P("groups", None, None))
    return jax.shard_map(body, mesh=mesh, in_specs=in_specs, out_specs=out_specs, check_vma=False)
```

profile of v0, /device:TPU:0, one launch (start us, length us, event | category | flops | bytes accessed | tf_op | source)
XLA Modules:
  0.0 56.4 jit_solution(18229373019059362458)
XLA Ops:
  0.6 0.8 %copy.11 = s32[1,1,4,3]{3,2,1,0:T(4,128)S(1)} copy(s32[1,1,4,3]{2,1,3,0:T(1,128)} %param.11) | data formatting | bytes 96 | tf_op args[4]
  1.4 0.1 reshape.13
  1.5 0.8 %copy.12 = s32[1,1,4,3]{3,2,1,0:T(4,128)S(1)} copy(s32[1,1,4,3]{2,1,3,0:T(1,128)} %param.12) | data formatting | bytes 96 | tf_op args[5]
  2.2 0.1 reshape.14
  2.3 1.2 %pad_add_fusion.route = s32[1,30]{1,0:T(1,128)} fusion(s32[1,6]{1,0:T(1,128)} %bitcast.1, s32[1,12]{1,0:T(1,128)S(1)} %reshape.14, s32[1,12]{1,0:T(1,128)S(1)} %reshape.13), kind=kLoop, calls=%fused_computation | loop fusion | flops 60 | bytes 240 | tf_op jit(solution)/shard_map/concatenate | solution.py:459
  3.6 49.0 %shard_map.86 = (f32[2,2,256,512]{3,2,1,0:T(8,128)}, f32[2,128,128]{2,1,0:T(8,128)}) custom-call(f32[2,2,256,512]{3,2,1,0:T(8,128)} %obj.1, f32[2,128,128]{2,1,0:T(8,128)} %probe.1, f32[6,128,128]{2,1,0:T(8,128)} %measured.1, s32[1,30]{1,0:T(1,128)} %pad_add_fusion.route, bf16[4,2,256,256]{3,2,1,0:T(8,128)(2,1)} %constant.2.clone.tabs), custom_call_target="tpu_custom_call" | custom-call | tf_op jit(solution)/shard_map/pallas_call | solution.py:463
  52.6 0.0 copy-start
  52.6 3.1 %copy.15 = f32[2,2,256,512]{3,2,1,0:T(8,128)} copy(f32[2,2,256,512]{3,2,1,0:T(8,128)} %get-tuple-element.4) | data formatting | bytes 4194304
  55.8 0.0 copy-done
  55.8 0.7 %copy.16 = f32[2,128,128]{2,1,0:T(8,128)} copy(f32[2,128,128]{2,1,0:T(8,128)S(1)} %copy-done) | data formatting | bytes 262144
Async XLA Ops:
  52.6 3.1 %copy-start = (f32[2,128,128]{2,1,0:T(8,128)S(1)}, f32[2,128,128]{2,1,0:T(8,128)}, u32[]{:S(2)}) copy-start(f32[2,128,128]{2,1,0:T(8,128)} %get-tuple-element.5) | copy-start | bytes 393220
where the time goes:
time: 56.6 us; the launch traced here: 56.4 us
  Pallas kernels  49 us (87%)
  local copies, waits for them, and re-layouts  5.48 us (10%)
  other arithmetic  1.24 us (2%)
  between operations  0.65 us (1%)
    pallas_call x1, Pallas kernels, body(): pl.pallas_call(functools.partial(kernel, n_tx, n_ty, n_sl, cap, positions...  49 us
    unnamed x6, local copies, waits for them, and re-layouts  5.31 us
    concatenate x1, other arithmetic, body(): jnp.concatenate([list_rows.reshape(1, -1), list_cols.reshape(1, -1), owne...  1.24 us

commit v1 on v0

--- a/solution.py
+++ b/solution.py
@@ -107,7 +107,7 @@
 
 def kernel(
     n_tx, n_ty, n_sl, cap, all_positions,
-    obj, probe, measured, route, tabs,
+    obj, probe, measured, list_r, list_c, owner, tabs,
     obj_out, probe_out,
     tile, pat, staged, cut_r, cut_c, put_r, put_c, patches, phis, grads, g_recv, placed,
     pieces, pg_mine, delta_mine, deltas, wave, pg_sum,
@@ -147,7 +147,7 @@
         seen = jnp.int32(0)
         found = [jnp.int32(-1)] * cap
         for p in range(positions):
-            here = route[0, 2 * n_tx * cap + p] == o
+            here = owner[0, p] == o
             for k in range(cap):
                 found[k] = jnp.where(here & (seen == k), jnp.int32(p), found[k])
             seen = seen + jnp.where(here, 1, 0)
@@ -202,7 +202,7 @@
 
     def slot_corner(t, c):
         s, k = c * half + t // cap, t % cap
-        return route[0, s * cap + k], route[0, (n_tx + s) * cap + k]
+        return list_r[k, 0, s], list_c[k, 0, s]
 
     def hot(shape, axis, shift):
         long = lax.broadcasted_iota(jnp.int32, shape, axis)
@@ -456,17 +456,17 @@
     devices = n_tx * n_ty * n_sl
     deep = 2 * px // delta_count(devices, 2 * px)
     tabs = jnp.asarray(real_tables(px))
-    route = jnp.concatenate([list_rows.reshape(1, -1), list_cols.reshape(1, -1), owner_row.reshape(1, -1)], axis=1)
+    tables = [jnp.transpose(one, (0, 3, 1, 2)).reshape(cap, 1, n_tx) for one in (list_rows, list_cols)]
     vmem = pl.BlockSpec(memory_space=pltpu.VMEM)
     smem = pl.BlockSpec(memory_space=pltpu.SMEM)
     dma = pltpu.SemaphoreType.DMA
     return pl.pallas_call(
         functools.partial(kernel, n_tx, n_ty, n_sl, cap, positions * n_tx * n_ty),
         out_shape=(
-            jax.ShapeDtypeStruct(object_field.shape, F32),
-            jax.ShapeDtypeStruct(probe_wave.shape, F32),
+            pltpu.VMEM(object_field.shape, F32),
+            pltpu.VMEM(probe_wave.shape, F32),
         ),
-        in_specs=[vmem, vmem, vmem, smem, vmem],
+        in_specs=[vmem, vmem, vmem, smem, smem, smem, vmem],
         out_specs=(vmem, vmem),
         scratch_shapes=[
             pltpu.VMEM((ITERS, total, 2, rows, cols), BF16),
@@ -501,7 +501,7 @@
         compiler_params=pltpu.CompilerParams(
             collective_id=0, has_side_effects=True, vmem_limit_bytes=58 * 2**20
         ),
-    )(object_field, probe_wave, measured, route, tabs)
+    )(object_field, probe_wave, measured, *tables, owner_row.reshape(1, -1), tabs)
 
 
 def solution(mesh):

time: 56.6 us -> 50.7 us (0.90)
  local copies, waits for them, and re-layouts: 5.48 us -> 1.98 us
  other arithmetic: 1.24 us -> 0 us
  Pallas kernels: 49 us -> 47.9 us
    unnamed x6 -> x2, local copies, waits for them, and re-layouts: 5.31 us -> 1.98 us
    concatenate x1 -> x0, other arithmetic: 1.24 us -> none  [body(): jnp.concatenate([list_rows.reshape(1, -1), list_cols.reshape(1, -1), owne...]
    pallas_call x1, Pallas kernels: 49 us -> 47.9 us  [body(): pl.pallas_call(functools.partial(kernel, n_tx, n_ty, n_sl, cap, positions...]
where the time goes in v1:
time: 50.7 us; the launch traced here: 50.6 us
  Pallas kernels  47.9 us (94%)
  local copies, waits for them, and re-layouts  1.98 us (4%)
  between operations  0.64 us (1%)
    pallas_call x1, Pallas kernels, body(): pl.pallas_call(functools.partial(kernel, n_tx, n_ty, n_sl, cap, positions...  47.9 us
    unnamed x2, local copies, waits for them, and re-layouts  1.98 us

profile of v1, /device:TPU:0, one launch (start us, length us, event | category | flops | bytes accessed | tf_op | source)
XLA Modules:
  0.0 50.6 jit_solution(10287107167247127043)
XLA Ops:
  0.6 47.9 %shard_map.86 = (f32[2,2,256,512]{3,2,1,0:T(8,128)S(1)}, f32[2,128,128]{2,1,0:T(8,128)S(1)}) custom-call(f32[2,2,256,512]{3,2,1,0:T(8,128)} %obj.1, f32[2,128,128]{2,1,0:T(8,128)} %probe.1, f32[6,128,128]{2,1,0:T(8,128)} %measured.1, s32[3,1,4]{2,1,0:T(1,128)} %bitcast.7, s32[3,1,4]{2,1,0:T(1,128)} %bitcast.8, s32[1,6]{1,0:T(1,128)} %bitcast.9, ...), custom_call_target="tpu_custom_call" | custom-call | tf_op jit(solution)/shard_map/pallas_call | solution.py:463
  48.6 1.3 %copy.11 = f32[2,2,256,512]{3,2,1,0:T(8,128)} copy(f32[2,2,256,512]{3,2,1,0:T(8,128)S(1)} %get-tuple-element.2) | data formatting | bytes 4194304
  49.9 0.7 %copy.12 = f32[2,128,128]{2,1,0:T(8,128)} copy(f32[2,128,128]{2,1,0:T(8,128)S(1)} %get-tuple-element.3) | data formatting | bytes 262144

commit v2 on v1

v2 whole, which is shorter than its diff:
```python
import functools
import math

import jax
import jax.numpy as jnp
import numpy as np
from jax import lax
from jax.experimental import pallas as pl
from jax.experimental.pallas import tpu as pltpu
from jax.sharding import PartitionSpec as P

ITERS = 2
PHASE = 0.25
STEP_OBJECT = 0.01
STEP_PROBE = 0.6
F32 = jnp.float32
BF16 = jnp.bfloat16
MESH = pl.DeviceIdType.MESH


def real_tables(pixels):
    index = np.arange(pixels)
    four = np.exp(-2j * math.pi * ((index[:, None] * index[None, :]) % pixels) / pixels) / math.sqrt(pixels)
    freq = np.where(index < pixels // 2, index, index - pixels).astype(np.float64)
    kern = (np.conj(four) * np.exp(-1j * PHASE * freq * freq / pixels)[None, :]) @ four
    found = []
    for matrix in (kern, four):
        right = np.block([[matrix.real, matrix.imag], [-matrix.imag, matrix.real]])
        found += [right, right.T]
    whole = np.stack(found).astype(np.float32)
    high = whole.astype(jnp.bfloat16)
    low = (whole - high.astype(np.float32)).astype(jnp.bfloat16)
    return np.stack([high, low], axis=1)


def split(x):
    high = x.astype(BF16)
    return high, (x - high.astype(F32)).astype(BF16)


def dot(a, b):
    return jnp.dot(a, b, preferred_element_type=F32)


def loop(count, step):
    if count <= 8:
        for i in range(count):
            step(i)
    else:
        lax.fori_loop(0, count, lambda i, carry: (step(i), carry)[1], 0)


def lanes(i, width):
    return pl.ds(i * width if isinstance(i, int) else pl.multiple_of(i * width, width), width)


def both_sides(x, tabs, right, left, px, fine=True):
    count = x.shape[1] // px

    def rows(v):
        return jnp.concatenate(
            [
                jnp.concatenate([v[:px, s * px : (s + 1) * px], v[px:, s * px : (s + 1) * px]], axis=1)
                for s in range(count)
            ],
            axis=0,
        )

    def columns(v):
        return jnp.concatenate(
            [
                jnp.concatenate([v[s * px : (s + 1) * px, :px], v[s * px : (s + 1) * px, px:]], axis=0)
                for s in range(count)
            ],
            axis=1,
        )

    m_high, m_low = tabs[right, 0], tabs[right, 1]
    if not fine:
        v = rows(x.astype(BF16))
        y = dot(jnp.concatenate([v, v], axis=1), jnp.concatenate([m_high, m_low], axis=0))
        v = columns(y.astype(BF16))
        m_high, m_low = tabs[left, 0], tabs[left, 1]
        return dot(jnp.concatenate([m_high, m_low], axis=1), jnp.concatenate([v, v], axis=0))
    high, low = split(x)
    high, low = rows(high), rows(low)
    y = dot(
        jnp.concatenate([high, low, high], axis=1), jnp.concatenate([m_high, m_high, m_low], axis=0)
    )
    high, low = split(y)
    high, low = columns(high), columns(low)
    m_high, m_low = tabs[left, 0], tabs[left, 1]
    return dot(
        jnp.concatenate([m_high, m_high, m_low], axis=1), jnp.concatenate([high, low, high], axis=0)
    )


def times(a, b, px):
    ar, ai, br, bi = a[:px], a[px:], b[:px], b[px:]
    return jnp.concatenate([ar * br - ai * bi, ar * bi + ai * br], axis=0)


def conj_times(a, g, px):
    ar, ai, gr, gi = a[:px], a[px:], g[:px], g[px:]
    return jnp.concatenate([ar * gr + ai * gi, ar * gi - ai * gr], axis=0)


def kernel(
    n_tx, n_ty, n_sl, cap, all_positions,
    obj, probe, measured, list_r, list_c, owner, tabs,
    obj_out, probe_out,
    field, pat, staged, cut_c, put_c, patches, away, phis, grads, g_recv, lifted, placed,
    pieces, pg_mine, zone, deltas, wave, pg_sum,
    load_sem, pat_send, pat_recv, p_send, p_recv, g_send, g_rcv, pc_send, pc_recv, zn_send, zn_recv, dl_send, dl_recv,
):
    ix, iy, core = lax.axis_index("tx"), lax.axis_index("ty"), lax.axis_index("sl")
    layers, _, rows, cols = obj.shape
    positions, px, _ = measured.shape
    half = n_tx // n_sl
    slots = half * cap
    total = n_sl * layers
    other = 1 - core
    plane = n_ty * n_sl
    flat = iy * n_sl + core
    deep = 2 * px // plane
    peer = {"sl": other}

    def beside(d):
        i = lax.rem(flat + d, plane)
        return i, {"ty": i // n_sl, "sl": lax.rem(i, n_sl)}

    def along(d):
        i = lax.rem(ix + d, n_tx)
        return i, {"tx": i}

    def load(q):
        return [
            pltpu.make_async_copy(obj.at[q // 2, q % 2, :, lanes(j, px)], field.at[q, j], load_sem.at[q, j])
            for j in range(cols // px)
        ]

    for q in range(2 * layers):
        for copy in load(q):
            copy.start()

    barrier = pltpu.get_barrier_semaphore()
    for d in range(1, plane):
        pl.semaphore_signal(barrier, inc=1, device_id=beside(d)[1], device_id_type=MESH)
    for d in range(1, n_tx):
        pl.semaphore_signal(barrier, inc=1, device_id=along(d)[1], device_id_type=MESH)

    wave[...] = jnp.concatenate([probe[0], probe[1]], axis=0)

    def stage(o, carry):
        seen = jnp.int32(0)
        found = [jnp.int32(-1)] * cap
        for p in range(positions):
            here = owner[0, p] == o
            for k in range(cap):
                found[k] = jnp.where(here & (seen == k), jnp.int32(p), found[k])
            seen = seen + jnp.where(here, 1, 0)
        for k in range(cap):
            values = jnp.full((px, px), -1.0, F32)
            for p in range(positions):
                values = jnp.where(found[k] == p, measured[p], values)
            staged[o, k] = values.astype(BF16)
        return carry

    lax.fori_loop(0, n_tx, stage, 0)

    def slot_corner(t, c):
        s, k = c * half + t // cap, t % cap
        return jnp.clip(list_r[k, 0, s], 0, rows - px), jnp.clip(list_c[k, 0, s], 0, cols - px)

    def hot(shape, axis, shift):
        long = lax.broadcasted_iota(jnp.int32, shape, axis)
        short = lax.broadcasted_iota(jnp.int32, shape, 1 - axis)
        return jnp.where(long - short == shift, 1.0, 0.0).astype(BF16)

    def column_block(col):
        return jnp.minimum(col // px, cols // px - 2)

    def build_cut(t):
        for at, c in ((t, core), (slots + t, other)):
            _, col = slot_corner(t, c)
            cut_c[at] = hot((2 * px, px), 0, col - column_block(col) * px)

    loop(slots, build_cut)
    for q in range(2 * layers):
        for copy in load(q):
            copy.wait()
    pl.semaphore_wait(barrier, plane - 1 + n_tx - 1)

    mine_sends = (ix // half) == core
    local_s = lax.rem(ix, half)

    def pattern_copy(o, s):
        return pltpu.make_async_remote_copy(
            src_ref=staged.at[o], dst_ref=pat.at[s], send_sem=pat_send.at[o], recv_sem=pat_recv.at[s],
            device_id={"tx": o}, device_id_type=MESH,
        )

    @pl.when(mine_sends)
    def _():
        for d in range(1, n_tx):
            pattern_copy(along(d)[0], local_s).start()
        pat[local_s] = staged[ix]

    def patch_copy(t):
        return pltpu.make_async_remote_copy(
            src_ref=away.at[:, :, lanes(t, px)],
            dst_ref=patches.at[pl.ds(core * layers, layers), :, lanes(t, px)],
            send_sem=p_send.at[t], recv_sem=p_recv.at[t], device_id=peer, device_id_type=MESH,
        )

    def grad_copy(it):
        return pltpu.make_async_remote_copy(
            src_ref=grads.at[pl.ds(other * layers, layers)], dst_ref=g_recv,
            send_sem=g_send.at[it], recv_sem=g_rcv.at[it], device_id=peer, device_id_type=MESH,
        )

    def piece_copy(it, d):
        i, where = beside(d)
        return pltpu.make_async_remote_copy(
            src_ref=pg_mine.at[it, pl.ds(pl.multiple_of(i * deep, deep), deep)], dst_ref=pieces.at[it, d],
            send_sem=pc_send.at[it, d], recv_sem=pc_recv.at[it, d], device_id=where, device_id_type=MESH,
        )

    def zone_copy(it, d):
        return pltpu.make_async_remote_copy(
            src_ref=zone.at[it, ix], dst_ref=zone.at[it, ix],
            send_sem=zn_send.at[it, d], recv_sem=zn_recv.at[it, d], device_id=along(d)[1], device_id_type=MESH,
        )

    own_rows = pl.ds(pl.multiple_of(flat * deep, deep), deep)

    def delta_copy(it, d):
        return pltpu.make_async_remote_copy(
            src_ref=deltas.at[it, own_rows], dst_ref=deltas.at[it, own_rows],
            send_sem=dl_send.at[it, d], recv_sem=dl_recv.at[it, d], device_id=beside(d)[1], device_id_type=MESH,
        )

    def plane_sum(it):
        add = pg_mine[it, own_rows].astype(F32)
        for d in range(1, plane):
            piece_copy(it, d).wait_recv()
            add = add + pieces[it, d].astype(F32)
        zone[it, ix] = add.astype(BF16)
        for d in range(1, n_tx):
            zone_copy(it, d).start()

    def whole_sum(it):
        for d in range(1, n_tx):
            zone_copy(it, d).wait_recv()
        add = zone[it, 0].astype(F32)
        for i in range(1, n_tx):
            add = add + zone[it, i].astype(F32)
        deltas[it, own_rows] = add.astype(BF16)
        for d in range(1, plane):
            delta_copy(it, d).start()

    def finish_probe(it):
        for d in range(1, plane):
            delta_copy(it, d).wait_recv()
        wave[...] -= (STEP_PROBE / all_positions) * deltas[it].astype(F32)

    def cut(it, t, c, at):
        row, col = slot_corner(t, c)
        first = column_block(col)
        held = jnp.concatenate(
            [
                jnp.concatenate(
                    [field[q, first + j, pl.ds(row, px), :].astype(BF16) for j in range(2)], axis=1
                )
                for q in range(2 * layers)
            ],
            axis=0,
        )
        return dot(held, cut_c[at]).astype(BF16)

    def build_put(t):
        _, col = slot_corner(t, core)
        put_c[lanes(t, px), :] = hot((px, cols), 1, col)
        _, col = slot_corner(t, other)
        put_c[lanes(slots + t, px), :] = hot((px, cols), 1, col)
        blank = jnp.zeros((rows - px, px), F32)
        for q in range(2 * layers):
            lifted[t, q, pl.ds(0, rows - px), :] = blank
            lifted[t, q, pl.ds(rows, rows - px), :] = blank

    chunk = max(d for d in range(1, 7) if slots % d == 0)
    fine_chunk = 2 if chunk % 2 == 0 else 1
    width = fine_chunk * px

    for it in range(ITERS):
        def cut_away(t):
            if it > 0:
                patch_copy(t).wait_send()
            done = cut(it, t, other, slots + t)
            for q in range(2 * layers):
                away[q // 2, q % 2 * px : (q % 2 + 1) * px, lanes(t, px)] = done[q * px : (q + 1) * px]
            patch_copy(t).start()

        def cut_own(t):
            done = cut(it, t, core, t)
            for q in range(2 * layers):
                patches[core * layers + q // 2, q % 2 * px : (q % 2 + 1) * px, lanes(t, px)] = (
                    done[q * px : (q + 1) * px]
                )

        loop(slots, cut_away)
        loop(slots, cut_own)
        if it == 0:
            loop(slots, build_put)
        if it > 0:
            finish_probe(it - 1)
        loop(slots, lambda t: patch_copy(t).wait_recv())

        def wait_patterns():
            def arrive(i, carry):
                @pl.when(core * half + i != ix)
                def _():
                    pattern_copy(ix, i).wait_recv()

                return carry

            lax.fori_loop(0, half, arrive, 0)

        if it == 0:
            wait_patterns()

        pg_sum[...] = jnp.zeros_like(pg_sum)

        def run(k):
            first = k * chunk
            spans = [lanes(first // fine_chunk + i, width) for i in range(chunk // fine_chunk)]
            w = jnp.concatenate([wave[...]] * fine_chunk, axis=1)
            psi = [times(w, patches[0, :, span].astype(F32), px) for span in spans]
            for l in range(1, total):
                for i, span in enumerate(spans):
                    phi = both_sides(psi[i], tabs, 0, 1, px)
                    phis[l - 1, :, span] = phi
                    psi[i] = times(phi, patches[l, :, span].astype(F32), px)
            g = []
            for i in range(len(spans)):
                far = both_sides(psi[i], tabs, 2, 3, px)
                target = []
                for s in range(fine_chunk):
                    t = first + i * fine_chunk + s
                    target.append(pat[t // cap, t % cap].astype(F32))
                target = jnp.concatenate(target, axis=1)
                fr, fi = far[:px], far[px:]
                miss = jnp.where(target >= 0.0, 2.0 * (fr * fr + fi * fi - target), 0.0)
                g.append(jnp.concatenate([miss * fr, miss * fi], axis=0))
            g = [both_sides(one, tabs, 3, 2, px, fine=False) for one in g]
            for l in range(total - 1, -1, -1):
                for i, span in enumerate(spans):
                    before = phis[l - 1, :, span] if l else w
                    grads[l, :, span] = conj_times(before, g[i], px).astype(BF16)
                    g[i] = conj_times(patches[l, :, span].astype(F32), g[i], px)
                    if l:
                        g[i] = both_sides(g[i], tabs, 1, 0, px, fine=False)
            for one in g:
                for s in range(fine_chunk):
                    pg_sum[...] += one[:, s * px : (s + 1) * px]

        if it > 0:
            grad_copy(it - 1).wait_send()
        loop(slots // chunk, run)

        pg_mine[it] = pg_sum[...].astype(BF16)
        for d in range(1, plane):
            piece_copy(it, d).start()
        grad_copy(it).start()

        def place(source, first, base, c, last):
            def lift(t):
                for q in range(2 * layers):
                    lifted[t, q, pl.ds(rows - px, px), :] = (
                        source[first + q // 2, q % 2 * px : (q % 2 + 1) * px, lanes(t, px)].astype(F32)
                    )

            def spread(t):
                row, _ = slot_corner(t, c)
                for q in range(2 * layers):
                    placed[q, :, lanes(base + t, px)] = lifted[t, q, pl.ds(rows - px - row, rows), :].astype(BF16)

            loop(slots, lift)
            loop(slots, spread)
            span = pl.ds(base * px, slots * px)
            for q in range(2 * layers):
                add = STEP_OBJECT * dot(placed[q, :, span], put_c[span, :])
                for j in range(cols // px):
                    now = field[q, j] - add[:, j * px : (j + 1) * px]
                    if last:
                        obj_out[q // 2, q % 2, :, lanes(j, px)] = now
                    else:
                        field[q, j] = now

        place(grads, core * layers, 0, core, False)
        plane_sum(it)
        grad_copy(it).wait_recv()
        place(g_recv, 0, slots, other, it == ITERS - 1)
        whole_sum(it)

    finish_probe(ITERS - 1)
    probe_out[0] = wave[:px]
    probe_out[1] = wave[px:]

    @pl.when(mine_sends)
    def _():
        for d in range(1, n_tx):
            pattern_copy(along(d)[0], local_s).wait_send()

    loop(slots, lambda t: patch_copy(t).wait_send())
    grad_copy(ITERS - 1).wait_send()
    for it in range(ITERS):
        for d in range(1, plane):
            piece_copy(it, d).wait_send()
            delta_copy(it, d).wait_send()
        for d in range(1, n_tx):
            zone_copy(it, d).wait_send()


def body(object_field, probe_wave, measured, owner_row, list_rows, list_cols):
    layers, _, rows, cols = object_field.shape
    positions, px, _ = measured.shape
    n_tx, n_ty, n_sl = lax.axis_size("tx"), lax.axis_size("ty"), lax.axis_size("sl")
    cap = list_rows.shape[-1]
    half = n_tx // n_sl
    slots = half * cap
    total = n_sl * layers
    plane = n_ty * n_sl
    deep = 2 * px // plane
    tabs = jnp.asarray(real_tables(px))
    tables = [jnp.transpose(one, (0, 3, 1, 2)).reshape(cap, 1, n_tx) for one in (list_rows, list_cols)]
    vmem = pl.BlockSpec(memory_space=pltpu.VMEM)
    smem = pl.BlockSpec(memory_space=pltpu.SMEM)
    dma = pltpu.SemaphoreType.DMA
    return pl.pallas_call(
        functools.partial(kernel, n_tx, n_ty, n_sl, cap, positions * n_tx * n_ty),
        out_shape=(
            pltpu.VMEM(object_field.shape, F32),
            pltpu.VMEM(probe_wave.shape, F32),
        ),
        in_specs=[pl.BlockSpec(memory_space=pl.ANY), vmem, vmem, smem, smem, smem, vmem],
        out_specs=(vmem, vmem),
        scratch_shapes=[
            pltpu.VMEM((2 * layers, cols // px, rows, px), F32),
            pltpu.VMEM((half, cap, px, px), BF16),
            pltpu.VMEM((n_tx, cap, px, px), BF16),
            pltpu.VMEM((2 * slots, 2 * px, px), BF16),
            pltpu.VMEM((2 * slots * px, cols), BF16),
            pltpu.VMEM((total, 2 * px, slots * px), BF16),
            pltpu.VMEM((layers, 2 * px, slots * px), BF16),
            pltpu.VMEM((total - 1, 2 * px, slots * px), F32),
            pltpu.VMEM((total, 2 * px, slots * px), BF16),
            pltpu.VMEM((layers, 2 * px, slots * px), BF16),
            pltpu.VMEM((slots, 2 * layers, 2 * rows - px, px), F32),
            pltpu.VMEM((2 * layers, rows, 2 * slots * px), BF16),
            pltpu.VMEM((ITERS, plane, deep, px), BF16),
            pltpu.VMEM((ITERS, 2 * px, px), BF16),
            pltpu.VMEM((ITERS, n_tx, deep, px), BF16),
            pltpu.VMEM((ITERS, 2 * px, px), BF16),
            pltpu.VMEM((2 * px, px), F32),
            pltpu.VMEM((2 * px, px), F32),
            dma((2 * layers, cols // px)),
            dma((n_tx,)),
            dma((half,)),
            dma((slots,)),
            dma((slots,)),
            dma((ITERS,)),
            dma((ITERS,)),
            dma((ITERS, plane)),
            dma((ITERS, plane)),
            dma((ITERS, n_tx)),
            dma((ITERS, n_tx)),
            dma((ITERS, plane)),
            dma((ITERS, plane)),
        ],
        compiler_params=pltpu.CompilerParams(
            collective_id=0, has_side_effects=True, vmem_limit_bytes=58 * 2**20
        ),
    )(object_field, probe_wave, measured, *tables, owner_row.reshape(1, -1), tabs)


def solution(mesh):
    in_specs = (
        P(("groups", "sl"), None, "tx", "ty"),
        P("groups", None, None),
        P(("groups", "tx", "ty"), None, None),
        P(("groups", "tx", "ty"), None),
        P(("groups", "tx"), "ty", None, None),
        P(("groups", "tx"), "ty", None, None),
    )
    out_specs = (P(("groups", "sl"), None, "tx", "ty"), P("groups", None, None))
    return jax.shard_map(body, mesh=mesh, in_specs=in_specs, out_specs=out_specs, check_vma=False)
```

time: 50.7 us -> 45.6 us (0.90)
  Pallas kernels: 47.9 us -> 42.8 us
    pallas_call x1, Pallas kernels: 47.9 us -> 42.8 us  [body(): pl.pallas_call(functools.partial(kernel, n_tx, n_ty, n_sl, cap, positions...]
where the time goes in v2:
time: 45.6 us; the launch traced here: 45.4 us
  Pallas kernels  42.8 us (94%)
  local copies, waits for them, and re-layouts  1.98 us (4%)
  between operations  0.64 us (1%)
    pallas_call x1, Pallas kernels, body(): pl.pallas_call(functools.partial(kernel, n_tx, n_ty, n_sl, cap, positions...  42.8 us
    unnamed x2, local copies, waits for them, and re-layouts  1.98 us

profile of v2, /device:TPU:0, one launch (start us, length us, event | category | flops | bytes accessed | tf_op | source)
XLA Modules:
  0.0 45.4 jit_solution(4250971928200209841)
XLA Ops:
  0.6 42.8 %shard_map.86 = (f32[2,2,256,512]{3,2,1,0:T(8,128)S(1)}, f32[2,128,128]{2,1,0:T(8,128)S(1)}) custom-call(f32[2,2,256,512]{3,2,1,0:T(8,128)} %obj.1, f32[2,128,128]{2,1,0:T(8,128)} %probe.1, f32[6,128,128]{2,1,0:T(8,128)} %measured.1, s32[3,1,4]{2,1,0:T(1,128)} %bitcast.7, s32[3,1,4]{2,1,0:T(1,128)} %bitcast.8, s32[1,6]{1,0:T(1,128)} %bitcast.9, ...), custom_call_target="tpu_custom_call" | custom-call | tf_op jit(solution)/shard_map/pallas_call | solution.py:440
  43.5 1.3 %copy.11 = f32[2,2,256,512]{3,2,1,0:T(8,128)} copy(f32[2,2,256,512]{3,2,1,0:T(8,128)S(1)} %get-tuple-element.2) | data formatting | bytes 4194304
  44.8 0.7 %copy.12 = f32[2,128,128]{2,1,0:T(8,128)} copy(f32[2,128,128]{2,1,0:T(8,128)S(1)} %get-tuple-element.3) | data formatting | bytes 262144

commit v3 on v2

--- a/solution.py
+++ b/solution.py
@@ -13,6 +13,7 @@
 PHASE = 0.25
 STEP_OBJECT = 0.01
 STEP_PROBE = 0.6
+KERN_SCALE = 1.6465
 F32 = jnp.float32
 BF16 = jnp.bfloat16
 MESH = pl.DeviceIdType.MESH
@@ -24,7 +25,7 @@
     freq = np.where(index < pixels // 2, index, index - pixels).astype(np.float64)
     kern = (np.conj(four) * np.exp(-1j * PHASE * freq * freq / pixels)[None, :]) @ four
     found = []
-    for matrix in (kern, four):
+    for matrix in (KERN_SCALE * kern, math.sqrt(pixels) * four):
         right = np.block([[matrix.real, matrix.imag], [-matrix.imag, matrix.real]])
         found += [right, right.T]
     whole = np.stack(found).astype(np.float32)
@@ -54,8 +55,9 @@
     return pl.ds(i * width if isinstance(i, int) else pl.multiple_of(i * width, width), width)
 
 
-def both_sides(x, tabs, right, left, px, fine=True):
+def both_sides(x, tabs, right, left, px, passes):
     count = x.shape[1] // px
+    scale = 1.0 / px if right >= 2 else KERN_SCALE**-2
 
     def rows(v):
         return jnp.concatenate(
@@ -76,12 +78,15 @@
         )
 
     m_high, m_low = tabs[right, 0], tabs[right, 1]
-    if not fine:
+    n_high, n_low = tabs[left, 0], tabs[left, 1]
+    if passes == 1:
+        y = dot(rows(x.astype(BF16)), m_high)
+        return scale * dot(n_high, columns(y.astype(BF16)))
+    if passes == 2:
         v = rows(x.astype(BF16))
         y = dot(jnp.concatenate([v, v], axis=1), jnp.concatenate([m_high, m_low], axis=0))
         v = columns(y.astype(BF16))
-        m_high, m_low = tabs[left, 0], tabs[left, 1]
-        return dot(jnp.concatenate([m_high, m_low], axis=1), jnp.concatenate([v, v], axis=0))
+        return scale * dot(jnp.concatenate([n_high, n_low], axis=1), jnp.concatenate([v, v], axis=0))
     high, low = split(x)
     high, low = rows(high), rows(low)
     y = dot(
@@ -89,9 +94,8 @@
     )
     high, low = split(y)
     high, low = columns(high), columns(low)
-    m_high, m_low = tabs[left, 0], tabs[left, 1]
-    return dot(
-        jnp.concatenate([m_high, m_high, m_low], axis=1), jnp.concatenate([high, low, high], axis=0)
+    return scale * dot(
+        jnp.concatenate([n_high, n_high, n_low], axis=1), jnp.concatenate([high, low, high], axis=0)
     )
 
 
@@ -107,11 +111,11 @@
 
 def kernel(
     n_tx, n_ty, n_sl, cap, all_positions,
-    obj, probe, measured, list_r, list_c, owner, tabs,
+    obj, probe, measured_at, list_r, list_c, owner, tabs_at,
     obj_out, probe_out,
-    field, pat, staged, cut_c, put_c, patches, away, phis, grads, g_recv, lifted, placed,
+    field, measured, tabs, pat, staged, cut_c, put_c, patches, away, phis, grads, g_recv, lifted, placed,
     pieces, pg_mine, zone, deltas, wave, pg_sum,
-    load_sem, pat_send, pat_recv, p_send, p_recv, g_send, g_rcv, pc_send, pc_recv, zn_send, zn_recv, dl_send, dl_recv,
+    load_sem, in_sem, pat_send, pat_recv, p_send, p_recv, g_send, g_rcv, pc_send, pc_recv, zn_send, zn_recv, dl_send, dl_recv,
 ):
     ix, iy, core = lax.axis_index("tx"), lax.axis_index("ty"), lax.axis_index("sl")
     layers, _, rows, cols = obj.shape
@@ -142,6 +146,11 @@
     for q in range(2 * layers):
         for copy in load(q):
             copy.start()
+
+    measured_load = pltpu.make_async_copy(measured_at, measured, in_sem.at[0])
+    tabs_load = pltpu.make_async_copy(tabs_at, tabs, in_sem.at[1])
+    measured_load.start()
+    tabs_load.start()
 
     barrier = pltpu.get_barrier_semaphore()
     for d in range(1, plane):
@@ -166,7 +175,6 @@
             staged[o, k] = values.astype(BF16)
         return carry
 
-    lax.fori_loop(0, n_tx, stage, 0)
 
     def slot_corner(t, c):
         s, k = c * half + t // cap, t % cap
@@ -186,6 +194,8 @@
             cut_c[at] = hot((2 * px, px), 0, col - column_block(col) * px)
 
     loop(slots, build_cut)
+    measured_load.wait()
+    lax.fori_loop(0, n_tx, stage, 0)
     for q in range(2 * layers):
         for copy in load(q):
             copy.wait()
@@ -291,8 +301,11 @@
     chunk = max(d for d in range(1, 7) if slots % d == 0)
     fine_chunk = 2 if chunk % 2 == 0 else 1
     width = fine_chunk * px
+    runs = slots // chunk
 
     for it in range(ITERS):
+        forth, back = (2, 1) if it == ITERS - 1 else (3, 2)
+
         def cut_away(t):
             if it > 0:
                 patch_copy(t).wait_send()
@@ -313,6 +326,7 @@
         if it == 0:
             loop(slots, build_put)
         if it > 0:
+            whole_sum(it - 1)
             finish_probe(it - 1)
         loop(slots, lambda t: patch_copy(t).wait_recv())
 
@@ -327,7 +341,9 @@
             lax.fori_loop(0, half, arrive, 0)
 
         if it == 0:
-            wait_patterns()
+            tabs_load.wait()
+            if runs > 8:
+                wait_patterns()
 
         pg_sum[...] = jnp.zeros_like(pg_sum)
 
@@ -338,12 +354,14 @@
             psi = [times(w, patches[0, :, span].astype(F32), px) for span in spans]
             for l in range(1, total):
                 for i, span in enumerate(spans):
-                    phi = both_sides(psi[i], tabs, 0, 1, px)
+                    phi = both_sides(psi[i], tabs, 0, 1, px, forth)
                     phis[l - 1, :, span] = phi
                     psi[i] = times(phi, patches[l, :, span].astype(F32), px)
+            if it == 0 and runs <= 8 and k == 0:
+                wait_patterns()
             g = []
             for i in range(len(spans)):
-                far = both_sides(psi[i], tabs, 2, 3, px)
+                far = both_sides(psi[i], tabs, 2, 3, px, forth)
                 target = []
                 for s in range(fine_chunk):
                     t = first + i * fine_chunk + s
@@ -352,21 +370,21 @@
                 fr, fi = far[:px], far[px:]
                 miss = jnp.where(target >= 0.0, 2.0 * (fr * fr + fi * fi - target), 0.0)
                 g.append(jnp.concatenate([miss * fr, miss * fi], axis=0))
-            g = [both_sides(one, tabs, 3, 2, px, fine=False) for one in g]
+            g = [both_sides(one, tabs, 3, 2, px, back) for one in g]
             for l in range(total - 1, -1, -1):
                 for i, span in enumerate(spans):
                     before = phis[l - 1, :, span] if l else w
                     grads[l, :, span] = conj_times(before, g[i], px).astype(BF16)
                     g[i] = conj_times(patches[l, :, span].astype(F32), g[i], px)
                     if l:
-                        g[i] = both_sides(g[i], tabs, 1, 0, px, fine=False)
+                        g[i] = both_sides(g[i], tabs, 1, 0, px, back)
             for one in g:
                 for s in range(fine_chunk):
                     pg_sum[...] += one[:, s * px : (s + 1) * px]
 
         if it > 0:
             grad_copy(it - 1).wait_send()
-        loop(slots // chunk, run)
+        loop(runs, run)
 
         pg_mine[it] = pg_sum[...].astype(BF16)
         for d in range(1, plane):
@@ -401,8 +419,8 @@
         plane_sum(it)
         grad_copy(it).wait_recv()
         place(g_recv, 0, slots, other, it == ITERS - 1)
-        whole_sum(it)
-
+
+    whole_sum(ITERS - 1)
     finish_probe(ITERS - 1)
     probe_out[0] = wave[:px]
     probe_out[1] = wave[px:]
@@ -435,6 +453,7 @@
     tabs = jnp.asarray(real_tables(px))
     tables = [jnp.transpose(one, (0, 3, 1, 2)).reshape(cap, 1, n_tx) for one in (list_rows, list_cols)]
     vmem = pl.BlockSpec(memory_space=pltpu.VMEM)
+    anywhere = pl.BlockSpec(memory_space=pl.ANY)
     smem = pl.BlockSpec(memory_space=pltpu.SMEM)
     dma = pltpu.SemaphoreType.DMA
     return pl.pallas_call(
@@ -443,10 +462,12 @@
             pltpu.VMEM(object_field.shape, F32),
             pltpu.VMEM(probe_wave.shape, F32),
         ),
-        in_specs=[pl.BlockSpec(memory_space=pl.ANY), vmem, vmem, smem, smem, smem, vmem],
+        in_specs=[anywhere, vmem, anywhere, smem, smem, smem, anywhere],
         out_specs=(vmem, vmem),
         scratch_shapes=[
             pltpu.VMEM((2 * layers, cols // px, rows, px), F32),
+            pltpu.VMEM(measured.shape, F32),
+            pltpu.VMEM(tabs.shape, BF16),
             pltpu.VMEM((half, cap, px, px), BF16),
             pltpu.VMEM((n_tx, cap, px, px), BF16),
             pltpu.VMEM((2 * slots, 2 * px, px), BF16),
@@ -465,6 +486,7 @@
             pltpu.VMEM((2 * px, px), F32),
             pltpu.VMEM((2 * px, px), F32),
             dma((2 * layers, cols // px)),
+            dma((2,)),
             dma((n_tx,)),
             dma((half,)),
             dma((slots,)),

time: 45.6 us -> 42.1 us (0.923)
  Pallas kernels: 42.8 us -> 39.4 us
    pallas_call x1, Pallas kernels: 42.8 us -> 39.4 us  [body(): pl.pallas_call(functools.partial(kernel, n_tx, n_ty, n_sl, cap, positions...]
where the time goes in v3:
time: 42.1 us; the launch traced here: 42 us
  Pallas kernels  39.4 us (94%)
  local copies, waits for them, and re-layouts  1.98 us (5%)
  between operations  0.64 us (2%)
    pallas_call x1, Pallas kernels, body(): pl.pallas_call(functools.partial(kernel, n_tx, n_ty, n_sl, cap, positions...  39.4 us
    unnamed x2, local copies, waits for them, and re-layouts  1.98 us

profile of v3, /device:TPU:0, one launch (start us, length us, event | category | flops | bytes accessed | tf_op | source)
XLA Modules:
  0.0 42.0 jit_solution(4677739543652623331)
XLA Ops:
  0.6 39.4 %shard_map.86 = (f32[2,2,256,512]{3,2,1,0:T(8,128)S(1)}, f32[2,128,128]{2,1,0:T(8,128)S(1)}) custom-call(f32[2,2,256,512]{3,2,1,0:T(8,128)} %obj.1, f32[2,128,128]{2,1,0:T(8,128)} %probe.1, f32[6,128,128]{2,1,0:T(8,128)} %measured_at.1, s32[3,1,4]{2,1,0:T(1,128)} %bitcast.7, s32[3,1,4]{2,1,0:T(1,128)} %bitcast.8, s32[1,6]{1,0:T(1,128)} %bitcast.9, ...), custom_call_target="tpu_custom_call" | custom-call | tf_op jit(solution)/shard_map/pallas_call | solution.py:459
  40.0 1.3 %copy.11 = f32[2,2,256,512]{3,2,1,0:T(8,128)} copy(f32[2,2,256,512]{3,2,1,0:T(8,128)S(1)} %get-tuple-element.2) | data formatting | bytes 4194304
  41.3 0.7 %copy.12 = f32[2,128,128]{2,1,0:T(8,128)} copy(f32[2,128,128]{2,1,0:T(8,128)S(1)} %get-tuple-element.3) | data formatting | bytes 262144

commit v4 on v3

--- a/solution.py
+++ b/solution.py
@@ -126,7 +126,7 @@
     other = 1 - core
     plane = n_ty * n_sl
     flat = iy * n_sl + core
-    deep = 2 * px // plane
+    deep = 2 * px // n_sl
     peer = {"sl": other}
 
     def beside(d):
@@ -136,6 +136,12 @@
     def along(d):
         i = lax.rem(ix + d, n_tx)
         return i, {"tx": i}
+
+    barrier = pltpu.get_barrier_semaphore()
+    for d in range(1, plane):
+        pl.semaphore_signal(barrier, inc=1, device_id=beside(d)[1], device_id_type=MESH)
+    for d in range(1, n_tx):
+        pl.semaphore_signal(barrier, inc=1, device_id=along(d)[1], device_id_type=MESH)
 
     def load(q):
         return [
@@ -151,14 +157,12 @@
     tabs_load = pltpu.make_async_copy(tabs_at, tabs, in_sem.at[1])
     measured_load.start()
     tabs_load.start()
-
-    barrier = pltpu.get_barrier_semaphore()
-    for d in range(1, plane):
-        pl.semaphore_signal(barrier, inc=1, device_id=beside(d)[1], device_id_type=MESH)
-    for d in range(1, n_tx):
-        pl.semaphore_signal(barrier, inc=1, device_id=along(d)[1], device_id_type=MESH)
-
-    wave[...] = jnp.concatenate([probe[0], probe[1]], axis=0)
+    probe_loads = [
+        pltpu.make_async_copy(probe.at[part], wave.at[pl.ds(part * px, px)], in_sem.at[2 + part]) for part in range(2)
+    ]
+    for copy in probe_loads:
+        copy.start()
+
 
     def stage(o, carry):
         seen = jnp.int32(0)
@@ -212,7 +216,7 @@
 
     @pl.when(mine_sends)
     def _():
-        for d in range(1, n_tx):
+        for d in range(n_tx - 1, 0, -1):
             pattern_copy(along(d)[0], local_s).start()
         pat[local_s] = staged[ix]
 
@@ -229,10 +233,13 @@
             send_sem=g_send.at[it], recv_sem=g_rcv.at[it], device_id=peer, device_id_type=MESH,
         )
 
+    own_rows = pl.ds(pl.multiple_of(core * deep, deep), deep)
+
     def piece_copy(it, d):
         i, where = beside(d)
+        theirs = pl.ds(pl.multiple_of(lax.rem(i, n_sl) * deep, deep), deep)
         return pltpu.make_async_remote_copy(
-            src_ref=pg_mine.at[it, pl.ds(pl.multiple_of(i * deep, deep), deep)], dst_ref=pieces.at[it, d],
+            src_ref=pg_mine.at[it, theirs], dst_ref=pieces.at[it, flat],
             send_sem=pc_send.at[it, d], recv_sem=pc_recv.at[it, d], device_id=where, device_id_type=MESH,
         )
 
@@ -242,19 +249,19 @@
             send_sem=zn_send.at[it, d], recv_sem=zn_recv.at[it, d], device_id=along(d)[1], device_id_type=MESH,
         )
 
-    own_rows = pl.ds(pl.multiple_of(flat * deep, deep), deep)
-
-    def delta_copy(it, d):
+    def delta_copy(it):
         return pltpu.make_async_remote_copy(
             src_ref=deltas.at[it, own_rows], dst_ref=deltas.at[it, own_rows],
-            send_sem=dl_send.at[it, d], recv_sem=dl_recv.at[it, d], device_id=beside(d)[1], device_id_type=MESH,
+            send_sem=dl_send.at[it], recv_sem=dl_recv.at[it], device_id=peer, device_id_type=MESH,
         )
 
     def plane_sum(it):
-        add = pg_mine[it, own_rows].astype(F32)
+        pieces[it, flat] = pg_mine[it, own_rows]
         for d in range(1, plane):
             piece_copy(it, d).wait_recv()
-            add = add + pieces[it, d].astype(F32)
+        add = pieces[it, 0].astype(F32)
+        for i in range(1, plane):
+            add = add + pieces[it, i].astype(F32)
         zone[it, ix] = add.astype(BF16)
         for d in range(1, n_tx):
             zone_copy(it, d).start()
@@ -265,14 +272,12 @@
         add = zone[it, 0].astype(F32)
         for i in range(1, n_tx):
             add = add + zone[it, i].astype(F32)
-        deltas[it, own_rows] = add.astype(BF16)
-        for d in range(1, plane):
-            delta_copy(it, d).start()
+        deltas[it, own_rows] = add
+        delta_copy(it).start()
 
     def finish_probe(it):
-        for d in range(1, plane):
-            delta_copy(it, d).wait_recv()
-        wave[...] -= (STEP_PROBE / all_positions) * deltas[it].astype(F32)
+        delta_copy(it).wait_recv()
+        wave[...] -= (STEP_PROBE / all_positions) * deltas[it]
 
     def cut(it, t, c, at):
         row, col = slot_corner(t, c)
@@ -342,6 +347,8 @@
 
         if it == 0:
             tabs_load.wait()
+            for copy in probe_loads:
+                copy.wait()
             if runs > 8:
                 wait_patterns()
 
@@ -435,9 +442,9 @@
     for it in range(ITERS):
         for d in range(1, plane):
             piece_copy(it, d).wait_send()
-            delta_copy(it, d).wait_send()
         for d in range(1, n_tx):
             zone_copy(it, d).wait_send()
+        delta_copy(it).wait_send()
 
 
 def body(object_field, probe_wave, measured, owner_row, list_rows, list_cols):
@@ -449,7 +456,7 @@
     slots = half * cap
     total = n_sl * layers
     plane = n_ty * n_sl
-    deep = 2 * px // plane
+    deep = 2 * px // n_sl
     tabs = jnp.asarray(real_tables(px))
     tables = [jnp.transpose(one, (0, 3, 1, 2)).reshape(cap, 1, n_tx) for one in (list_rows, list_cols)]
     vmem = pl.BlockSpec(memory_space=pltpu.VMEM)
@@ -462,7 +469,7 @@
             pltpu.VMEM(object_field.shape, F32),
             pltpu.VMEM(probe_wave.shape, F32),
         ),
-        in_specs=[anywhere, vmem, anywhere, smem, smem, smem, anywhere],
+        in_specs=[anywhere, anywhere, anywhere, smem, smem, smem, anywhere],
         out_specs=(vmem, vmem),
         scratch_shapes=[
             pltpu.VMEM((2 * layers, cols // px, rows, px), F32),
@@ -482,11 +489,11 @@
             pltpu.VMEM((ITERS, plane, deep, px), BF16),
             pltpu.VMEM((ITERS, 2 * px, px), BF16),
             pltpu.VMEM((ITERS, n_tx, deep, px), BF16),
-            pltpu.VMEM((ITERS, 2 * px, px), BF16),
+            pltpu.VMEM((ITERS, 2 * px, px), F32),
             pltpu.VMEM((2 * px, px), F32),
             pltpu.VMEM((2 * px, px), F32),
             dma((2 * layers, cols // px)),
-            dma((2,)),
+            dma((4,)),
             dma((n_tx,)),
             dma((half,)),
             dma((slots,)),
@@ -497,8 +504,8 @@
             dma((ITERS, plane)),
             dma((ITERS, n_tx)),
             dma((ITERS, n_tx)),
-            dma((ITERS, plane)),
-            dma((ITERS, plane)),
+            dma((ITERS,)),
+            dma((ITERS,)),
         ],
         compiler_params=pltpu.CompilerParams(
             collective_id=0, has_side_effects=True, vmem_limit_bytes=58 * 2**20

time: 42.1 us -> 39.7 us (0.943)
  Pallas kernels: 39.4 us -> 36.9 us
    pallas_call x1, Pallas kernels: 39.4 us -> 36.9 us  [body(): pl.pallas_call(functools.partial(kernel, n_tx, n_ty, n_sl, cap, positions...]
where the time goes in v4:
time: 39.7 us; the launch traced here: 39.5 us
  Pallas kernels  36.9 us (93%)
  local copies, waits for them, and re-layouts  1.98 us (5%)
  between operations  0.64 us (2%)
    pallas_call x1, Pallas kernels, body(): pl.pallas_call(functools.partial(kernel, n_tx, n_ty, n_sl, cap, positions...  36.9 us
    unnamed x2, local copies, waits for them, and re-layouts  1.98 us

profile of v4, /device:TPU:0, one launch (start us, length us, event | category | flops | bytes accessed | tf_op | source)
XLA Modules:
  0.0 39.5 jit_solution(2638318313713144725)
XLA Ops:
  0.6 36.9 %shard_map.86 = (f32[2,2,256,512]{3,2,1,0:T(8,128)S(1)}, f32[2,128,128]{2,1,0:T(8,128)S(1)}) custom-call(f32[2,2,256,512]{3,2,1,0:T(8,128)} %obj.1, f32[2,128,128]{2,1,0:T(8,128)} %probe.1, f32[6,128,128]{2,1,0:T(8,128)} %measured_at.1, s32[3,1,4]{2,1,0:T(1,128)} %bitcast.7, s32[3,1,4]{2,1,0:T(1,128)} %bitcast.8, s32[1,6]{1,0:T(1,128)} %bitcast.9, ...), custom_call_target="tpu_custom_call" | custom-call | tf_op jit(solution)/shard_map/pallas_call | solution.py:466
  37.5 1.3 %copy.11 = f32[2,2,256,512]{3,2,1,0:T(8,128)} copy(f32[2,2,256,512]{3,2,1,0:T(8,128)S(1)} %get-tuple-element.2) | data formatting | bytes 4194304
  38.9 0.7 %copy.12 = f32[2,128,128]{2,1,0:T(8,128)} copy(f32[2,128,128]{2,1,0:T(8,128)S(1)} %get-tuple-element.3) | data formatting | bytes 262144

commit v5 on v4

--- a/solution.py
+++ b/solution.py
@@ -111,9 +111,9 @@
 
 def kernel(
     n_tx, n_ty, n_sl, cap, all_positions,
-    obj, probe, measured_at, list_r, list_c, owner, tabs_at,
+    obj, probe, measured_at, list_r_at, list_c_at, owner_at, tabs_at,
     obj_out, probe_out,
-    field, measured, tabs, pat, staged, cut_c, put_c, patches, away, phis, grads, g_recv, lifted, placed,
+    list_r, list_c, owner, field, measured, tabs, pat, staged, cut_c, put_c, patches, away, phis, grads, g_recv, lifted, placed,
     pieces, pg_mine, zone, deltas, wave, pg_sum,
     load_sem, in_sem, pat_send, pat_recv, p_send, p_recv, g_send, g_rcv, pc_send, pc_recv, zn_send, zn_recv, dl_send, dl_recv,
 ):
@@ -143,6 +143,13 @@
     for d in range(1, n_tx):
         pl.semaphore_signal(barrier, inc=1, device_id=along(d)[1], device_id_type=MESH)
 
+    routing = [
+        pltpu.make_async_copy(source, kept, in_sem.at[4 + i])
+        for i, (source, kept) in enumerate(((list_c_at, list_c), (owner_at, owner), (list_r_at, list_r)))
+    ]
+    for copy in routing:
+        copy.start()
+
     def load(q):
         return [
             pltpu.make_async_copy(obj.at[q // 2, q % 2, :, lanes(j, px)], field.at[q, j], load_sem.at[q, j])
@@ -197,6 +204,8 @@
             _, col = slot_corner(t, c)
             cut_c[at] = hot((2 * px, px), 0, col - column_block(col) * px)
 
+    for copy in routing:
+        copy.wait()
     loop(slots, build_cut)
     measured_load.wait()
     lax.fori_loop(0, n_tx, stage, 0)
@@ -328,8 +337,6 @@
 
         loop(slots, cut_away)
         loop(slots, cut_own)
-        if it == 0:
-            loop(slots, build_put)
         if it > 0:
             whole_sum(it - 1)
             finish_probe(it - 1)
@@ -352,7 +359,8 @@
             if runs > 8:
                 wait_patterns()
 
-        pg_sum[...] = jnp.zeros_like(pg_sum)
+        if runs > 1:
+            pg_sum[...] = jnp.zeros_like(pg_sum)
 
         def run(k):
             first = k * chunk
@@ -385,18 +393,27 @@
                     g[i] = conj_times(patches[l, :, span].astype(F32), g[i], px)
                     if l:
                         g[i] = both_sides(g[i], tabs, 1, 0, px, back)
+            add = None
             for one in g:
                 for s in range(fine_chunk):
-                    pg_sum[...] += one[:, s * px : (s + 1) * px]
+                    part = one[:, s * px : (s + 1) * px]
+                    add = part if add is None else add + part
+            if runs == 1:
+                pg_mine[it] = add.astype(BF16)
+            else:
+                pg_sum[...] += add
 
         if it > 0:
             grad_copy(it - 1).wait_send()
         loop(runs, run)
 
-        pg_mine[it] = pg_sum[...].astype(BF16)
+        if runs > 1:
+            pg_mine[it] = pg_sum[...].astype(BF16)
         for d in range(1, plane):
             piece_copy(it, d).start()
         grad_copy(it).start()
+        if it == 0:
+            loop(slots, build_put)
 
         def place(source, first, base, c, last):
             def lift(t):
@@ -461,7 +478,6 @@
     tables = [jnp.transpose(one, (0, 3, 1, 2)).reshape(cap, 1, n_tx) for one in (list_rows, list_cols)]
     vmem = pl.BlockSpec(memory_space=pltpu.VMEM)
     anywhere = pl.BlockSpec(memory_space=pl.ANY)
-    smem = pl.BlockSpec(memory_space=pltpu.SMEM)
     dma = pltpu.SemaphoreType.DMA
     return pl.pallas_call(
         functools.partial(kernel, n_tx, n_ty, n_sl, cap, positions * n_tx * n_ty),
@@ -469,9 +485,12 @@
             pltpu.VMEM(object_field.shape, F32),
             pltpu.VMEM(probe_wave.shape, F32),
         ),
-        in_specs=[anywhere, anywhere, anywhere, smem, smem, smem, anywhere],
+        in_specs=[anywhere, anywhere, anywhere, anywhere, anywhere, anywhere, anywhere],
         out_specs=(vmem, vmem),
         scratch_shapes=[
+            pltpu.SMEM(tables[0].shape, jnp.int32),
+            pltpu.SMEM(tables[1].shape, jnp.int32),
+            pltpu.SMEM((1, positions), jnp.int32),
             pltpu.VMEM((2 * layers, cols // px, rows, px), F32),
             pltpu.VMEM(measured.shape, F32),
             pltpu.VMEM(tabs.shape, BF16),
@@ -493,7 +512,7 @@
             pltpu.VMEM((2 * px, px), F32),
             pltpu.VMEM((2 * px, px), F32),
             dma((2 * layers, cols // px)),
-            dma((4,)),
+            dma((7,)),
             dma((n_tx,)),
             dma((half,)),
             dma((slots,)),

time: 39.7 us -> 39.1 us (0.985)
  Pallas kernels: 36.9 us -> 36.2 us
    pallas_call x1, Pallas kernels: 36.9 us -> 36.2 us  [body(): pl.pallas_call(functools.partial(kernel, n_tx, n_ty, n_sl, cap, positions...]
where the time goes in v5:
time: 39.1 us; the launch traced here: 38.9 us
  Pallas kernels  36.2 us (93%)
  local copies, waits for them, and re-layouts  1.98 us (5%)
  between operations  0.64 us (2%)
    pallas_call x1, Pallas kernels, body(): pl.pallas_call(functools.partial(kernel, n_tx, n_ty, n_sl, cap, positions...  36.2 us
    unnamed x2, local copies, waits for them, and re-layouts  1.98 us

profile of v5, /device:TPU:0, one launch (start us, length us, event | category | flops | bytes accessed | tf_op | source)
XLA Modules:
  0.0 38.9 jit_solution(17665707553363517467)
XLA Ops:
  0.6 36.2 %shard_map.86 = (f32[2,2,256,512]{3,2,1,0:T(8,128)S(1)}, f32[2,128,128]{2,1,0:T(8,128)S(1)}) custom-call(f32[2,2,256,512]{3,2,1,0:T(8,128)} %obj.1, f32[2,128,128]{2,1,0:T(8,128)} %probe.1, f32[6,128,128]{2,1,0:T(8,128)} %measured_at.1, s32[3,1,4]{2,1,0:T(1,128)} %bitcast.7, s32[3,1,4]{2,1,0:T(1,128)} %bitcast.8, s32[1,6]{1,0:T(1,128)} %bitcast.9, ...), custom_call_target="tpu_custom_call" | custom-call | tf_op jit(solution)/shard_map/pallas_call | solution.py:482
  36.9 1.3 %copy.11 = f32[2,2,256,512]{3,2,1,0:T(8,128)} copy(f32[2,2,256,512]{3,2,1,0:T(8,128)S(1)} %get-tuple-element.2) | data formatting | bytes 4194304
  38.2 0.7 %copy.12 = f32[2,128,128]{2,1,0:T(8,128)} copy(f32[2,128,128]{2,1,0:T(8,128)S(1)} %get-tuple-element.3) | data formatting | bytes 262144

commit v6 on v5

--- a/solution.py
+++ b/solution.py
@@ -376,7 +376,7 @@
                 wait_patterns()
             g = []
             for i in range(len(spans)):
-                far = both_sides(psi[i], tabs, 2, 3, px, forth)
+                far = both_sides(psi[i], tabs, 2, 3, px, 1 if it == ITERS - 1 else forth)
                 target = []
                 for s in range(fine_chunk):
                     t = first + i * fine_chunk + s

time: 39.1 us -> 39 us (level)
  no operation moved by 1% of the time
where the time goes in v6:
time: 39 us; the launch traced here: 38.8 us
  Pallas kernels  36.2 us (93%)
  local copies, waits for them, and re-layouts  1.98 us (5%)
  between operations  0.64 us (2%)
    pallas_call x1, Pallas kernels, body(): pl.pallas_call(functools.partial(kernel, n_tx, n_ty, n_sl, cap, positions...  36.2 us
    unnamed x2, local copies, waits for them, and re-layouts  1.98 us

profile of v6, /device:TPU:0, one launch (start us, length us, event | category | flops | bytes accessed | tf_op | source)
XLA Modules:
  0.0 38.8 jit_solution(15119564454927797757)
XLA Ops:
  0.6 36.2 %shard_map.86 = (f32[2,2,256,512]{3,2,1,0:T(8,128)S(1)}, f32[2,128,128]{2,1,0:T(8,128)S(1)}) custom-call(f32[2,2,256,512]{3,2,1,0:T(8,128)} %obj.1, f32[2,128,128]{2,1,0:T(8,128)} %probe.1, f32[6,128,128]{2,1,0:T(8,128)} %measured_at.1, s32[3,1,4]{2,1,0:T(1,128)} %bitcast.7, s32[3,1,4]{2,1,0:T(1,128)} %bitcast.8, s32[1,6]{1,0:T(1,128)} %bitcast.9, ...), custom_call_target="tpu_custom_call" | custom-call | tf_op jit(solution)/shard_map/pallas_call | solution.py:482
  36.8 1.3 %copy.11 = f32[2,2,256,512]{3,2,1,0:T(8,128)} copy(f32[2,2,256,512]{3,2,1,0:T(8,128)S(1)} %get-tuple-element.2) | data formatting | bytes 4194304
  38.2 0.7 %copy.12 = f32[2,128,128]{2,1,0:T(8,128)} copy(f32[2,128,128]{2,1,0:T(8,128)S(1)} %get-tuple-element.3) | data formatting | bytes 262144
